TPU v7x, 256 devices: a whole 4x4x8 slice. The times are simulated.
256 devices in a mesh: dp: 128 (over z, y_lo, x, core), group: 2 (over y_hi).
Axes of the slice: x: 4, y: 4 (y_hi: 2, y_lo: 2; y = y_hi * 2 + y_lo), z: 8, core: 2. Of those that a mesh axis runs over, the one named last changes fastest.
Arguments:
- atom_feats: bfloat16 [2048, 32, 512], P(('dp', 'group')), may hold values from -6 to 6
- coords: float32 [2048, 3, 32], P(('dp', 'group')), may hold values from -6 to 6
- atom_counts: int32 [2048], P(('dp', 'group')), may hold values from 8 to 32
- positives: int32 [2048], P(('dp', 'group')), may hold values from 0 to 2047, each once
- z2: bfloat16 [2048, 128], P(('dp', 'group')), may hold values from -6 to 6
- w_qkv: bfloat16 [512, 1536], replicated, may hold values from -0.25 to 0.25
- w_out: bfloat16 [512, 512], replicated, may hold values from -0.25 to 0.25
- proj: bfloat16 [512, 128], replicated, may hold values from -0.25 to 0.25
- bias_weight: float32 [128, 64], replicated, may hold values from -2 to 36
- ln_gain: float32 [512], replicated, may hold values from 0.5 to 1.5
Outputs:
- loss: float32 [], replicated
- grad_z2: float32 [2048, 128], P(('dp', 'group'))
- grad_w_qkv: float32 [512, 1536], replicated
- grad_w_out: float32 [512, 512], replicated
- grad_proj: float32 [512, 128], replicated
- grad_bias_weight: float32 [128, 64], replicated
- grad_ln_gain: float32 [512], replicated
Inputs may be any that keep to these rules, and one draw needn't show every extreme that they name: positives is a permutation of the 2048 molecules.
All inputs are finite; a program needn't handle non-finite values.
Results may differ from a plain program's by a relative error of at most 0.014.
Values may be sent and summed in bfloat16 or wider, within the bound.
A program may use at most 128 MiB of HBM per device.

v0:
```python
import math
import jax
import jax.numpy as jnp
from jax import lax
from jax.sharding import PartitionSpec as P


def pair_distance(coords):
    offsets = coords[:, :, :, None] - coords[:, :, None, :]
    return jnp.sqrt(jnp.sum(offsets * offsets, axis=1) + 0.25)


def kernel_values(distance, kernels):
    centers = jnp.arange(kernels).astype(jnp.float32) * (12.0 / kernels)
    return jnp.exp(-(((distance[..., None] - centers) / 0.5) ** 2))


def group_split(values, width):
    return values.reshape((values.shape[0] // width, width) + values.shape[1:])


def bias_forward(distance, bias_weight):
    mol_count = distance.shape[0]
    width = math.gcd(mol_count, 8)

    def one_group(group_distance):
        basis = kernel_values(group_distance, bias_weight.shape[0])
        return jnp.einsum("mijk,kh->mhij", basis, bias_weight, precision=lax.Precision.HIGHEST)

    biased = lax.map(one_group, group_split(distance, width))
    return biased.reshape((mol_count,) + biased.shape[2:])


def bias_backward(distance, bias_slope, kernels):
    width = math.gcd(distance.shape[0], 8)

    def add_group(running, pieces):
        basis = kernel_values(pieces[0], kernels)
        return (
            running
            + jnp.einsum("mijk,mhij->kh", basis, pieces[1], precision=lax.Precision.HIGHEST),
            None,
        )

    start_sum = jnp.zeros((kernels, bias_slope.shape[1]), jnp.float32)
    summed, unused = lax.scan(
        add_group, start_sum, (group_split(distance, width), group_split(bias_slope, width))
    )
    return summed


def encode_core(params_in, pair_bias, feats, counts):
    w_qkv, w_out, proj, ln_gain = params_in
    mol_count, atom_count, model_width = feats.shape
    head_count = pair_bias.shape[1]
    head_dim = model_width // head_count
    inputs = feats.astype(jnp.float32)
    center = jnp.mean(inputs, axis=-1, keepdims=True)
    spread = jnp.mean((inputs - center) ** 2, axis=-1, keepdims=True)
    normed = ((inputs - center) * lax.rsqrt(spread + 1e-05) * ln_gain).astype(jnp.bfloat16)
    projected = jnp.dot(
        normed.reshape(mol_count * atom_count, model_width),
        w_qkv,
        preferred_element_type=jnp.float32,
    ).astype(jnp.bfloat16)
    projected = projected.reshape(mol_count, atom_count, 3, head_count, head_dim)
    query_heads = projected[:, :, 0]
    key_heads = projected[:, :, 1]
    value_heads = projected[:, :, 2]
    scores = (
        jnp.einsum("mihd,mjhd->mhij", query_heads, key_heads, preferred_element_type=jnp.float32)
        * head_dim ** (-0.5)
        + pair_bias
    )
    is_valid = jnp.arange(atom_count)[None, :] < counts[:, None]
    scores = jnp.where(is_valid[:, None, None, :], scores, -1e30)
    highest = jnp.max(scores, axis=-1, keepdims=True)
    expo = jnp.exp(scores - highest)
    attn_weights = (expo / jnp.sum(expo, axis=-1, keepdims=True)).astype(jnp.bfloat16)
    context = jnp.einsum(
        "mhij,mjhd->mihd", attn_weights, value_heads, preferred_element_type=jnp.float32
    ).astype(jnp.bfloat16)
    hidden = inputs + jnp.dot(
        context.reshape(mol_count * atom_count, model_width),
        w_out,
        preferred_element_type=jnp.float32,
    ).reshape(mol_count, atom_count, model_width)
    pooled = jnp.sum(jnp.where(is_valid[..., None], hidden, 0.0), axis=1)
    return jnp.dot(pooled.astype(jnp.bfloat16), proj, preferred_element_type=jnp.float32)


def unit_rows(values):
    inverse = lax.rsqrt(jnp.mean(values * values, axis=1, keepdims=True) + 1e-06) * values.shape[
        1
    ] ** (-0.5)
    return (values * inverse, inverse)


def unit_backward(values, inverse, grad):
    along = jnp.sum(values * grad, axis=1, keepdims=True)
    return inverse * (grad - values * along * (inverse * inverse))


def on_device(
    atom_feats, coords, atom_counts, positives, z2, w_qkv, w_out, proj, bias_weight, ln_gain
):
    distance = pair_distance(coords)
    pair_bias = bias_forward(distance, bias_weight)

    def local_encode(params_in, bias_in):
        return encode_core(params_in, bias_in, atom_feats, atom_counts)

    z3, pullback = jax.vjp(local_encode, (w_qkv, w_out, proj, ln_gain), pair_bias)
    unit, inverse = unit_rows(z3)
    z3_half = unit.astype(jnp.bfloat16)
    z2_all = lax.all_gather(z2, ("dp", "group"), axis=0, tiled=True)
    batch_rows = z2_all.shape[0]
    logits = jnp.dot(z3_half, z2_all.T, preferred_element_type=jnp.float32)
    expo = jnp.exp(logits)
    row_lse = jnp.log(jnp.sum(expo, axis=1))
    columns = jnp.arange(batch_rows)
    is_positive = positives[:, None] == columns[None, :]
    positive_score = jnp.sum(jnp.where(is_positive, logits, 0.0), axis=1)
    local_sum = jnp.sum(0.5 * row_lse - positive_score)
    col_total = lax.psum(jnp.sum(expo, axis=0), ("dp", "group"))
    col_lse = jnp.log(col_total)
    column_part = 0.5 * jnp.sum(col_lse)
    slope = (
        0.5 * jnp.exp(logits - row_lse[:, None])
        + 0.5 * jnp.exp(logits - col_lse[None, :])
        - is_positive.astype(jnp.float32)
    ).astype(jnp.bfloat16)
    grad_z2 = lax.psum_scatter(
        lax.dot_general(
            slope, z3_half, (((0,), (0,)), ((), ())), preferred_element_type=jnp.float32
        ),
        ("dp", "group"),
        scatter_dimension=0,
        tiled=True,
    )
    grad_unit = jnp.dot(slope, z2_all, preferred_element_type=jnp.float32)
    grad_z3 = unit_backward(z3, inverse, grad_unit)
    pieces, bias_slope = pullback(grad_z3)
    grad_bias = bias_backward(distance, bias_slope, bias_weight.shape[0])
    totals = lax.psum(
        (
            local_sum,
            pieces[0].astype(jnp.float32),
            pieces[1].astype(jnp.float32),
            pieces[2].astype(jnp.float32),
            grad_bias,
            pieces[3],
        ),
        ("dp", "group"),
    )
    loss = (totals[0] + column_part) / batch_rows
    return (loss, grad_z2, totals[1], totals[2], totals[3], totals[4], totals[5])


def solution(mesh):
    return jax.shard_map(
        on_device,
        mesh=mesh,
        in_specs=(
            P(("dp", "group"), None, None),
            P(("dp", "group"), None, None),
            P(("dp", "group")),
            P(("dp", "group")),
            P(("dp", "group"), None),
            P(),
            P(),
            P(),
            P(),
            P(),
        ),
        out_specs=(P(), P(("dp", "group"), None), P(), P(), P(), P(), P()),
        check_vma=False,
    )
```

profile of v0, /device:TPU:97, one launch (start us, length us, event | category | flops | bytes accessed | tf_op | source)
XLA Modules:
  0.0 1103.0 jit_solution(12725409746250518894)
XLA Ops:
  7.2 1.2 convert_reduce_fusion.1
  8.4 1.2 fusion.44
  9.6 1.1 fusion.42
  10.7 0.7 copy-done.13
  12.3 2.8 reshape.179
  15.1 3.9 fusion.58
  19.5 0.6 copy-done.21
  20.1 5.4 fusion.10
  25.5 9.2 copy.77
  34.7 7.3 fusion.60
  41.9 2.7 fusion.9
  45.2 2.3 divide_convert_fusion
  47.5 1.2 convolution_convert_fusion.4
  49.9 569.9 %all_gather.3 = bf16[2048,128]{1,0:T(8,128)(2,1)S(1)} all-gather(bf16[8,128]{1,0:T(8,128)(2,1)S(1)} %copy-done.25), channel_id=1, replica_groups=mesh['dp'=128,'group'=2] {'dp','group'}, dimensions={0}, use_global_device_ids=true | all-gather | bytes 526336 | tf_op jit(solution)/shard_map/all_gather | solution.py:116
  619.8 0.8 copy-done.12
  621.1 130.1 %psum.50 = f32[2048]{0:T(1024)S(1)} all-reduce(f32[2048]{0:T(1024)S(1)} %get-tuple-element.27), channel_id=1, replica_groups=mesh['dp'=128,'group'=2] {'dp','group'}, use_global_device_ids=true, to_apply=%region_12.13 | all-reduce | flops 2048 | bytes 16384 | tf_op jit(solution)/shard_map/psum | solution.py:125
  751.7 0.6 fusion.59
  752.3 1.4 multiply_reduce_fusion.1
  753.7 1.0 fusion.32
  754.7 1.1 fusion.34
  755.9 0.8 multiply_divide_fusion
  756.6 0.8 broadcast_select_fusion
  757.5 2.1 fusion.61
  759.6 1.8 copy.80
  761.4 2.4 reshape.180
  763.8 5.9 fusion.21
  769.8 5.8 fusion.3
  775.7 8.8 convert_reduce_fusion
  784.5 6.1 add_select_fusion
  790.6 3.7 fusion.25
  794.4 2.2 fusion.22
  796.5 1.4 fusion.53
  798.0 1.2 copy.87
  799.2 0.7 reshape.182
  799.9 2.7 pad_add_fusion
  802.6 5.3 copy.86
  807.9 4.3 reshape.181
  812.2 2.3 fusion.14
  814.5 1.3 fusion.28
  815.8 0.6 fusion.43
  816.4 8.8 copy.88
  825.2 10.3 fusion.33
  835.5 74.4 %all-reduce.4 = (f32[]{:T(128)}, f32[128,64]{0,1:T(8,128)}, f32[512]{0:T(512)}) all-reduce(f32[]{:T(128)} %get-tuple-element.52, f32[128,64]{0,1:T(8,128)S(1)} %fusion.33, f32[512]{0:T(512)S(1)} %fusion.43), channel_id=1, replica_groups=mesh['dp'=128,'group'=2] {'dp','group'}, use_global_device_ids=true, to_apply=%region_10.11 | all-reduce | flops 8705 | bytes 69640 | tf_op jit(solution)/shard_map/psum | solution.py:145
  911.2 176.8 %all-reduce.8.cloned.1.call-done = (f32[2048,128]{1,0:T(8,128)}, f32[512,1536]{1,0:T(8,128)}, f32[512,512]{1,0:T(8,128)}, f32[512,128]{1,0:T(8,128)}) async-done(((f32[2048,128]{1,0:T(8,128)}, f32[512,1536]{1,0:T(8,128)}, f32[512,512]{1,0:T(8,128)}, f32[512,128]{1,0:T(8,128)}), (f32[2048,128]{1,0:T(8,128)}, f32[512,1536]{1,0:T(8,128)}, f32[512,512]{1,0:T(8,128)}, ...) | async-done | bytes 5505040
  1088.0 1.4 constant_dynamic-slice_fusion
  1089.3 3.8 copy.126
  1093.1 1.0 copy.127
  1094.1 0.7 copy.128
  (79 shorter events, 4.4 us)
Async XLA Ops:
  7.2 4.3 copy-start
  7.2 1080.8 %all-reduce.8.cloned.1.call-start = ((), (), s32[]{:S(2)}) async-start(), calls=%async_computation | async-start | bytes 11010048
  10.7 0.7 copy-start.13
  12.3 6.8 copy-start.27
  12.3 6.9 copy-start.23
  15.1 5.0 copy-start.26
  19.5 0.6 copy-start.21
  41.9 3.2 copy-start.1
  45.2 2.3 copy-start.9
  47.4 572.4 %copy-start.3 = (bf16[8,64,32,32]{2,3,1,0:T(8,128)(2,1)}, bf16[8,64,32,32]{2,3,1,0:T(8,128)(2,1)S(1)}, u32[]{:S(2)}) copy-start(bf16[8,64,32,32]{2,3,1,0:T(8,128)(2,1)S(1)} %divide_convert_fusion) | copy-start | bytes 3145732
  47.4 1.3 copy-start.11
  47.5 1.7 copy-start.15
  47.5 2.1 copy-start.20
  47.5 2.4 copy-start.25
  47.5 573.1 %copy-start.24 = (s32[8]{0:T(128)S(1)}, s32[8]{0:T(128)}, u32[]{:S(2)}) copy-start(s32[8]{0:T(128)} %param.13) | copy-start | bytes 100
  49.1 570.7 %copy-start.6 = (bf16[8,64,8,32]{3,2,1,0:T(8,128)(2,1)}, bf16[8,64,8,32]{3,2,1,0:T(8,128)(2,1)S(1)}, u32[]{:S(2)}) copy-start(bf16[8,64,8,32]{3,2,1,0:T(8,128)(2,1)S(1)} %convolution_convert_fusion.4) | copy-start | bytes 786436
  619.8 0.8 copy-start.12
  763.8 5.9 copy-start.8
  763.8 5.9 copy-start.10
  763.8 5.9 copy-start.16
  763.8 11.8 %slice-start = ((s8[8388608]{0:T(1024)(128)(4,1)}), s8[4194304]{0:T(1024)(128)(4,1)S(1)}, s32[]{:S(2)}) async-start(s8[8388608]{0:T(1024)(128)(4,1)} %bitcast.90), calls=%async_computation.1 | async-start | bytes 8388608
  769.8 5.9 slice-start.1
  775.6 8.8 copy-start.4
  784.5 6.1 copy-start.5
  790.6 3.7 copy-start.2
  794.4 3.6 copy-start.7
  802.6 9.6 copy-start.14
  807.9 6.6 copy-start.18
  816.4 8.8 copy-start.22
  1088.0 5.2 copy-start.17
  1089.3 4.8 copy-start.19
Sparse Core Ops, SparseCore 0:
  815.9 272.0 all-reduce.7
where the time goes:
time: 1110 us; the launch traced here: 1100 us
  blocking collectives  774 us (70%)
  waiting for transfers between devices  177 us (16%)
  matrix products  54.6 us (5%)
  local copies, waits for them, and re-layouts  50.9 us (5%)
  other arithmetic  29.1 us (3%)
  between operations  17.1 us (2%)
    all_gather x1, blocking collectives, on_device(): z2_all = lax.all_gather(z2, ('dp', 'group'), axis=0, tiled=True)  570 us
    unnamed x2, waiting for transfers between devices  177 us
    psum x1, blocking collectives, on_device(): col_total = lax.psum(jnp.sum(expo, axis=0), ('dp', 'group'))  130 us
    psum x1, blocking collectives, on_device(): lax.psum((local_sum, pieces[0].astype(jnp.float32), pieces[1].astype(jnp....  74.4 us
  transfers between devices with their start and end apart: 1, of which 1 were waited for; matrix products, arithmetic and copies ran while one was open for 2% of the time, Pallas kernels for 0%

commit v1 on v0

--- a/solution.py
+++ b/solution.py
@@ -113,7 +113,10 @@
     z3, pullback = jax.vjp(local_encode, (w_qkv, w_out, proj, ln_gain), pair_bias)
     unit, inverse = unit_rows(z3)
     z3_half = unit.astype(jnp.bfloat16)
-    z2_all = lax.all_gather(z2, ("dp", "group"), axis=0, tiled=True)
+    z2_all = jnp.concatenate(
+        lax.all_to_all(jnp.stack([z2] * lax.axis_size(("dp", "group"))), ("dp", "group"), 0, 0),
+        axis=0,
+    )
     batch_rows = z2_all.shape[0]
     logits = jnp.dot(z3_half, z2_all.T, preferred_element_type=jnp.float32)
     expo = jnp.exp(logits)

time: 1110 us -> 508 us (0.46)
  blocking collectives: 774 us -> 151 us
  starting transfers between devices: 0.04 us -> 15.4 us
    all_gather x1 -> x0, blocking collectives: 570 us -> none  [on_device(): z2_all = lax.all_gather(z2, ('dp', 'group'), axis=0, tiled=True)]
    psum x1, blocking collectives: 130 us -> 77.5 us  [on_device(): col_total = lax.psum(jnp.sum(expo, axis=0), ('dp', 'group'))]
    all_to_all x0 -> x1, starting transfers between devices: none -> 15.3 us  [on_device(): lax.all_to_all(jnp.stack([z2] * lax.axis_size(('dp', 'group'))), ('dp', '...]
  transfers between devices with their start and end apart: 1 -> 2, of which waited for: 1 -> 1; matrix products, arithmetic and copies ran while one was open for 2% -> 14% of each run, Pallas kernels for 0% -> 0%
where the time goes in v1:
time: 508 us; the launch traced here: 504 us
  waiting for transfers between devices  177 us (35%)
  blocking collectives  151 us (30%)
  local copies, waits for them, and re-layouts  59.5 us (12%)
  matrix products  55.6 us (11%)
  other arithmetic  28.6 us (6%)
  between operations  17.2 us (3%)
  starting transfers between devices  15.4 us (3%)
    unnamed x2, waiting for transfers between devices  177 us
    psum x1, blocking collectives, on_device(): col_total = lax.psum(jnp.sum(expo, axis=0), ('dp', 'group'))  77.5 us
    psum x1, blocking collectives, on_device(): lax.psum((local_sum, pieces[0].astype(jnp.float32), pieces[1].astype(jnp....  73.6 us
    all_to_all x1, starting transfers between devices, on_device(): lax.all_to_all(jnp.stack([z2] * lax.axis_size(('dp', 'group'))), ('dp', '...  15.3 us
    dot_general x3, matrix products, encode_core(): jnp.einsum('mhij,mjhd->mihd', attn_weights, value_heads, preferred_elemen...  13.9 us
    unnamed x71, local copies, waits for them, and re-layouts  11.7 us
    dot_general x3, matrix products, encode_core(): jnp.einsum('mihd,mjhd->mhij', query_heads, key_heads, preferred_element_t...  10.7 us
    dot_general x1, matrix products, add_group(): jnp.einsum('mijk,mhij->kh', basis, pieces[1], precision=lax.Precision.HIG...  10.3 us
  transfers between devices with their start and end apart: 2, of which 1 were waited for; matrix products, arithmetic and copies ran while one was open for 14% of the time, Pallas kernels for 0%

profile of v1, /device:TPU:97, one launch (start us, length us, event | category | flops | bytes accessed | tf_op | source)
XLA Modules:
  0.0 504.3 jit_solution(4086400112390075601)
XLA Ops:
  7.2 1.7 stack.2
  8.9 15.3 %all-to-all-start = ((bf16[256,8,128]{2,1,0:T(8,128)(2,1)}), bf16[256,8,128]{2,1,0:T(8,128)(2,1)}, u32[]{:S(2)}, u32[]{:S(2)}) async-start(bf16[256,8,128]{2,1,0:T(8,128)(2,1)} %stack.2), calls=%async_computation | async-start | bytes 1048576 | tf_op jit(solution)/shard_map/all_to_all | solution.py:117
  24.3 1.1 convert_reduce_fusion.1
  25.3 1.2 fusion.44
  26.5 1.1 fusion.42
  29.2 3.4 reshape.184
  32.6 3.9 fusion.60
  37.6 5.4 %fusion.10 = f32[8,32,32,64]{3,2,1,0:T(8,128)} fusion(f32[128,64]{0,1:T(8,128)S(1)} %copy-done.27, f32[128]{0:T(128)S(1)} %convert_multiply_fusion.1, f32[8,32,32]{2,0,1:T(8,128)S(1)} %copy.75), kind=kOutput, calls=%fused_computation.17 | convolution fusion | flops 809500672 | bytes 2163200 | tf_op jit(solution)/shard_map/while/body/eval_jaxpr/mijk,kh->mhij/dot_general | solution.py:28
  43.0 9.2 %copy.77 = f32[8,32,32,64]{1,2,3,0:T(8,128)} copy(f32[8,32,32,64]{3,2,1,0:T(8,128)} %fusion.10) | data formatting | bytes 4194304 | tf_op jit(solution)/shard_map/while/body/eval_jaxpr/mijk,kh->mhij/dot_general | solution.py:28
  52.2 7.3 %fusion.62 = (f32[8,64,32]{2,1,0:T(8,128)S(1)}, f32[8,64,32,32]{2,3,1,0:T(8,128)S(1)}) fusion(f32[8,32,32,64]{1,2,3,0:T(8,128)} %copy.77, bf16[8,32,1,64,8]{1,0,4,3,2:T(8,128)(2,1)S(1)} %get-tuple-element.46, bf16[8,32,1,64,8]{1,0,4,3,2:T(8,128)(2,1)} %get-tuple-element.45, pred[8,32]{1,0:T(8,128)(4,1)S(1)} %iota_compare_fusion.1), kind=kOutput, calls=%fused_computation.103 | convolution fusion | flops 10469376 | bytes 4784384 | tf_op jit(solution)/shard_map/jvp(mihd,mjhd->mhij)/dot_general | solution.py:71
  59.4 2.7 fusion.9
  62.6 2.3 divide_convert_fusion
  64.9 2.0 copy-done.3
  66.9 2.2 convolution_convert_fusion.4
  69.7 3.4 copy.87
  73.1 2.6 reshape.188
  75.7 1.8 fusion.31
  77.8 0.8 multiply_divide_fusion
  78.6 1.5 exponential_reduce_fusion
  80.0 77.5 %psum.50 = f32[2048]{0:T(1024)S(1)} all-reduce(f32[2048]{0:T(1024)S(1)} %get-tuple-element.27), channel_id=1, replica_groups=mesh['dp'=128,'group'=2] {'dp','group'}, use_global_device_ids=true, to_apply=%region_12.13 | all-reduce | flops 2048 | bytes 16384 | tf_op jit(solution)/shard_map/psum | solution.py:128
  158.8 1.4 multiply_reduce_fusion.1
  160.3 1.0 fusion.32
  161.2 1.1 fusion.34
  162.3 1.5 broadcast_select_fusion
  163.8 0.8 bitcast_select_fusion
  164.6 2.1 fusion.63
  166.7 1.8 copy.80
  168.5 2.4 reshape.186
  170.9 5.9 %fusion.21 = bf16[8,32,1,64,8]{1,4,3,0,2:T(8,128)(2,1)} fusion(bf16[8,64,32,32]{2,3,1,0:T(8,128)(2,1)} %copy-done.3, bf16[8,64,8,32]{3,0,2,1:T(8,128)(2,1)} %bitcast.100), kind=kOutput, calls=%fused_computation.32 | convolution fusion | flops 8519680 | bytes 1572864 | tf_op jit(solution)/shard_map/transpose(jvp(mhij,mjhd->mihd))/dot_general | solution.py:80
  176.8 5.8 %fusion.3 = (f32[8,64,32]{2,1,0:T(8,128)S(1)}, bf16[8,64,32,32]{2,3,1,0:T(8,128)(2,1)S(1)}) fusion(f32[8,64,32,32]{2,3,1,0:T(8,128)} %copy-done.1, f32[8,64,32]{2,1,0:T(8,128)S(1)} %copy-done.13, f32[8,64,32]{2,1,0:T(8,128)S(1)} %get-tuple-element.53, bf16[8,32,1,64,8]{1,0,4,3,2:T(8,128)(2,1)S(1)} %copy-done.8, bf16[8,64,8,32]{3,0,2,1:T(8,128)(2,1)S(1)} %bitcast.101), kind=kOutput, calls=%fused_computation.5 | convolution fusion | flops 11517952 | bytes 3866624 | tf_op jit(solution)/shard_map/transpose(jvp(mhij,mjhd->mihd))/dot_general | solution.py:80
  182.7 8.8 %convert_reduce_fusion = (f32[8,64,32]{2,1,0:T(8,128)S(1)}, pred[8,64,32,32]{2,3,1,0:T(8,128)(4,1)S(1)}, f32[8,64,32]{2,1,0:T(8,128)S(1)}) fusion(f32[8,64,32,32]{2,3,1,0:T(8,128)S(1)} %bitcast.98, f32[8,64,32]{2,1,0:T(8,128)S(1)} %get-tuple-element.53, f32[8,64,32]{2,1,0:T(8,128)S(1)} %neg.16, f32[8,64,32]{2,1,0:T(8,128)S(1)} %fusion.9, ...), kind=kLoop, calls=%fused_computation.9 | loop fusion | flops 4685824 | bytes 3997696 | tf_op jit(solution)/shard_map/jvp()/reduce_sum | solution.py:77
  191.6 6.1 %add_select_fusion = f32[8,64,32,32]{2,3,1,0:T(8,128)S(1)} fusion(pred[8,64,32,32]{2,3,1,0:T(8,128)(4,1)S(1)} %get-tuple-element.42, f32[8,64,32]{2,1,0:T(8,128)S(1)} %negate_divide_fusion, pred[8,32]{1,0:T(8,128)(4,1)S(1)} %copy-done.24, f32[8,64,32,32]{2,3,1,0:T(8,128)S(1)} %bitcast.98, f32[8,64,32]{2,1,0:T(8,128)S(1)} %get-tuple-element.53, ...), kind=kLoop, calls=%fused_computation.8 | loop fusion | flops 4194304 | bytes 6029568 | tf_op jit(solution)/shard_map/transpose(jvp(jit(_where)))/select_n | solution.py:76
  197.7 2.3 fusion.25
  200.0 0.9 copy-done.2
  200.9 1.2 fusion.22
  202.1 1.4 fusion.57
  203.5 0.8 pad_add_fusion
  204.4 5.3 %copy.86 = bf16[8,32,3,64,8]{1,0,4,3,2:T(8,128)(2,1)} copy(bf16[8,32,3,64,8]{1,4,3,0,2:T(8,128)(2,1)S(1)} %pad_add_fusion) | data formatting | bytes 1572864 | tf_op jit(solution)/shard_map/transpose(jvp())/add_any | solution.py:67
  209.7 4.1 reshape.187
  213.8 2.3 fusion.14
  216.1 1.3 fusion.28
  218.2 8.9 %copy.88 = f32[8,64,32,32]{1,3,0,2:T(8,128)} copy(f32[8,64,32,32]{2,3,1,0:T(8,128)} %copy-done.2) | data formatting | bytes 4194304 | tf_op jit(solution)/shard_map/transpose(jvp(jit(_where)))/select_n | solution.py:76
  227.1 10.3 %fusion.33 = f32[128,64]{0,1:T(8,128)S(1)} fusion(f32[8,64,32,32]{1,3,0,2:T(8,128)} %copy.88, f32[128]{0:T(128)S(1)} %copy-done.30, f32[8,32,32]{2,0,1:T(8,128)S(1)} %copy-done.20), kind=kOutput, calls=%fused_computation.45 | convolution fusion | flops 809500672 | bytes 2163200 | tf_op jit(solution)/shard_map/while/body/eval_jaxpr/mijk,mhij->kh/dot_general | solution.py:41
  237.4 73.6 %all-reduce.4 = (f32[]{:T(128)}, f32[128,64]{0,1:T(8,128)}, f32[512]{0:T(512)}) all-reduce(f32[]{:T(128)} %get-tuple-element.52, f32[128,64]{0,1:T(8,128)S(1)} %fusion.33, f32[512]{0:T(512)S(1)} %fusion.43), channel_id=1, replica_groups=mesh['dp'=128,'group'=2] {'dp','group'}, use_global_device_ids=true, to_apply=%region_10.11 | all-reduce | flops 8705 | bytes 69640 | tf_op jit(solution)/shard_map/psum | solution.py:148
  312.3 177.0 %all-reduce.8.cloned.1.call-done = (f32[2048,128]{1,0:T(8,128)}, f32[512,1536]{1,0:T(8,128)}, f32[512,512]{1,0:T(8,128)}, f32[512,128]{1,0:T(8,128)}) async-done(((f32[2048,128]{1,0:T(8,128)}, f32[512,1536]{1,0:T(8,128)}, f32[512,512]{1,0:T(8,128)}, f32[512,128]{1,0:T(8,128)}), (f32[2048,128]{1,0:T(8,128)}, f32[512,1536]{1,0:T(8,128)}, f32[512,512]{1,0:T(8,128)}, ...) | async-done | bytes 5505040
  489.3 1.4 constant_dynamic-slice_fusion
  490.7 3.8 copy.126
  494.5 1.0 copy.127
  (87 shorter events, 6.8 us)
Async XLA Ops:
  7.2 21.2 %copy-start = (bf16[512,1536]{1,0:T(8,128)(2,1)S(1)}, bf16[512,1536]{1,0:T(8,128)(2,1)}, u32[]{:S(2)}) copy-start(bf16[512,1536]{1,0:T(8,128)(2,1)} %param.15) | copy-start | bytes 4718596
  8.9 69.7 %all-to-all-start = ((bf16[256,8,128]{2,1,0:T(8,128)(2,1)}), bf16[256,8,128]{2,1,0:T(8,128)(2,1)}, u32[]{:S(2)}, u32[]{:S(2)}) async-start(bf16[256,8,128]{2,1,0:T(8,128)(2,1)} %stack.2), calls=%async_computation | async-start | bytes 1048576 | tf_op jit(solution)/shard_map/all_to_all | solution.py:117
  24.2 465.1 %all-reduce.8.cloned.1.call-start = ((), (), s32[]{:S(2)}) async-start(), calls=%async_computation.1 | async-start | bytes 11010048
  24.3 12.7 %copy-start.29 = (f32[128]{0:T(128)}, f32[128]{0:T(128)S(1)}, u32[]{:S(2)}) copy-start(f32[128]{0:T(128)S(1)} %convert_multiply_fusion.1) | copy-start | bytes 1540
  26.5 1.1 copy-start.21
  27.7 0.7 copy-start.11
  29.2 7.3 %copy-start.28 = (s32[8]{0:T(128)S(1)}, s32[8]{0:T(128)}, u32[]{:S(2)}) copy-start(s32[8]{0:T(128)} %param.12) | copy-start | bytes 100
  29.2 7.4 %copy-start.25 = (f32[8,3,32]{2,0,1:T(8,128)S(1)}, f32[8,3,32]{2,0,1:T(8,128)}, u32[]{:S(2)}) copy-start(f32[8,3,32]{2,0,1:T(8,128)} %param.11) | copy-start | bytes 9220
  32.6 5.0 copy-start.27
  36.6 39.1 %copy-start.23 = (pred[8,32]{1,0:T(8,128)(4,1)}, pred[8,32]{1,0:T(8,128)(4,1)S(1)}, u32[]{:S(2)}) copy-start(pred[8,32]{1,0:T(8,128)(4,1)S(1)} %iota_compare_fusion.1) | copy-start | bytes 772
  37.0 0.6 copy-start.19
  59.4 3.2 copy-start.1
  62.6 4.3 copy-start.7
  64.9 2.0 copy-start.3
  66.9 8.8 %copy-start.9 = (bf16[8,32,512]{2,1,0:T(8,128)(2,1)S(1)}, bf16[8,32,512]{2,1,0:T(8,128)(2,1)}, u32[]{:S(2)}) copy-start(bf16[8,32,512]{2,1,0:T(8,128)(2,1)} %param.10) | copy-start | bytes 786436
  69.1 8.5 %copy-start.18 = (bf16[512,128]{1,0:T(8,128)(2,1)S(1)}, bf16[512,128]{1,0:T(8,128)(2,1)}, u32[]{:S(2)}) copy-start(bf16[512,128]{1,0:T(8,128)(2,1)} %param.17) | copy-start | bytes 393220
  170.9 5.9 %copy-start.6 = (bf16[8,32,64,8]{1,0,3,2:T(8,128)(2,1)S(1)}, bf16[8,32,64,8]{1,0,3,2:T(8,128)(2,1)}, u32[]{:S(2)}) copy-start(bf16[8,32,64,8]{1,0,3,2:T(8,128)(2,1)} %reshape.186) | copy-start | bytes 786436
  170.9 5.9 %copy-start.8 = (bf16[8,32,1,64,8]{1,0,4,3,2:T(8,128)(2,1)S(1)}, bf16[8,32,1,64,8]{1,0,4,3,2:T(8,128)(2,1)}, u32[]{:S(2)}) copy-start(bf16[8,32,1,64,8]{1,0,4,3,2:T(8,128)(2,1)} %get-tuple-element.44) | copy-start | bytes 786436
  170.9 5.9 %copy-start.13 = (f32[8,64,32]{2,1,0:T(8,128)S(1)}, f32[8,64,32]{2,1,0:T(8,128)}, u32[]{:S(2)}) copy-start(f32[8,64,32]{2,1,0:T(8,128)} %multiply_divide_fusion) | copy-start | bytes 196612
  170.9 11.8 %slice-start = ((s8[8388608]{0:T(1024)(128)(4,1)}), s8[4194304]{0:T(1024)(128)(4,1)S(1)}, s32[]{:S(2)}) async-start(s8[8388608]{0:T(1024)(128)(4,1)} %bitcast.97), calls=%async_computation.2 | async-start | bytes 8388608
  176.8 5.9 %slice-start.1 = ((s8[8388608]{0:T(1024)(128)(4,1)}), s8[4194304]{0:T(1024)(128)(4,1)S(1)}, s32[]{:S(2)}) async-start(s8[8388608]{0:T(1024)(128)(4,1)} %bitcast.97), calls=%async_computation.3 | async-start | bytes 8388608
  182.7 8.8 %copy-start.4 = (bf16[8,64,32,32]{2,3,1,0:T(8,128)(2,1)}, bf16[8,64,32,32]{2,3,1,0:T(8,128)(2,1)S(1)}, u32[]{:S(2)}) copy-start(bf16[8,64,32,32]{2,3,1,0:T(8,128)(2,1)S(1)} %get-tuple-element.61) | copy-start | bytes 3145732
  182.7 8.8 %copy-start.24 = (pred[8,32]{1,0:T(8,128)(4,1)S(1)}, pred[8,32]{1,0:T(8,128)(4,1)}, u32[]{:S(2)}) copy-start(pred[8,32]{1,0:T(8,128)(4,1)} %copy-done.23) | copy-start | bytes 772
  191.6 6.1 %copy-start.5 = (bf16[8,32,1,64,8]{1,0,4,3,2:T(8,128)(2,1)S(1)}, bf16[8,32,1,64,8]{1,0,4,3,2:T(8,128)(2,1)}, u32[]{:S(2)}) copy-start(bf16[8,32,1,64,8]{1,0,4,3,2:T(8,128)(2,1)} %get-tuple-element.45) | copy-start | bytes 786436
  197.7 3.2 copy-start.2
  200.9 1.2 copy-start.26
  200.9 2.6 copy-start.10
  204.4 9.5 %copy-start.12 = (bf16[8,32,512]{2,1,0:T(8,128)(2,1)S(1)}, bf16[8,32,512]{2,1,0:T(8,128)(2,1)}, u32[]{:S(2)}) copy-start(bf16[8,32,512]{2,1,0:T(8,128)(2,1)} %copy-done.11) | copy-start | bytes 786436
  209.7 6.4 %copy-start.15 = (bf16[256,512]{0,1:T(8,128)(2,1)S(1)}, bf16[256,512]{0,1:T(8,128)(2,1)}, u32[]{:S(2)}) copy-start(bf16[256,512]{0,1:T(8,128)(2,1)} %reshape.188) | copy-start | bytes 786436
  209.7 6.4 %copy-start.16 = (bf16[8,32,512]{2,1,0:T(8,128)(2,1)S(1)}, bf16[8,32,512]{2,1,0:T(8,128)(2,1)}, u32[]{:S(2)}) copy-start(bf16[8,32,512]{2,1,0:T(8,128)(2,1)} %broadcast_select_fusion) | copy-start | bytes 786436
  216.1 1.4 copy-start.22
  218.1 9.0 %copy-start.20 = (f32[8,32,32]{2,0,1:T(8,128)S(1)}, f32[8,32,32]{2,0,1:T(8,128)}, u32[]{:S(2)}) copy-start(f32[8,32,32]{2,0,1:T(8,128)} %copy-done.19) | copy-start | bytes 98308
  218.1 9.0 %copy-start.30 = (f32[128]{0:T(128)S(1)}, f32[128]{0:T(128)}, u32[]{:S(2)}) copy-start(f32[128]{0:T(128)} %copy-done.29) | copy-start | bytes 1540
  489.3 5.2 %copy-start.14 = (f32[512,512]{1,0:T(8,128)S(1)}, f32[512,512]{1,0:T(8,128)}, u32[]{:S(2)}) copy-start(f32[512,512]{1,0:T(8,128)} %get-tuple-element.65) | copy-start | bytes 3145732
  490.7 4.8 copy-start.17
Sparse Core Ops, SparseCore 0:
  217.6 271.6 all-reduce.7
